TPU v7x, 32 devices: a whole 2x2x4 slice. The times are simulated.
32 devices in a mesh: groups: 2 (over y), wide: 4 (over z), narrow: 4 (over x, core).
Axes of the slice: x: 2, y: 2, z: 4, core: 2. Of those that a mesh axis runs over, the one named last changes fastest.
Arguments:
- tokens: bfloat16 [1536, 8192], P(('groups', 'wide'), 'narrow'), parts along dimension 0, may hold values from -6 to 6
- tenant_ids: int32 [768], P('wide'), may hold values from 0 to 1, as said below
- placement: int32 [4], replicated, may hold values from 0 to 1, as said below
- base_weight: bfloat16 [8192, 512], P(None, 'narrow'), may hold values from -0.0625 to 0.0625
- delta_levels: bfloat16 [4, 8192, 512], P('wide', None, 'narrow'), may hold values from -8 to 7, as said below
- delta_scales: float32 [4, 512], P('wide', 'narrow'), may hold values from 0.0005 to 0.002
- outlier_index: int32 [4, 128], P('wide'), may hold values from 0 to 8191, as said below
- outlier_values: bfloat16 [4, 128, 512], P('wide', None, 'narrow'), may hold values from -0.125 to 0.125
Outputs:
- adapted_out: bfloat16 [1536, 512], P(('groups', 'wide'), 'narrow'), parts along dimension 0
There are 2 independent parts, one for each index of `groups`. A program takes and returns all parts, laid end to end along the dimension named above; an argument that names none is the same for every part. Nothing has to cross between parts.
Inputs may be any that keep to these rules, and one draw needn't show every extreme that they name: `placement`: every tenant 0 to 1 is held by at least one index; several indices may hold the same tenant. `tenant_ids`: among the 192 rows of one index of wide, at most 120 name the same tenant, and in every such block some tenant is named by exactly 120 rows. `delta_levels`: whole numbers. Indices with equal placement entries hold equal delta_levels, delta_scales, outlier_index and outlier_values. `outlier_index`: each holder's list names 128 distinct features, among them feature 0 and feature 8192 - 1.
All inputs are finite; a program needn't handle non-finite values.
Results may differ from a plain program's by a relative error of at most 0.0039.
Values may be sent and summed in bfloat16 or wider, within the bound.
A program may use at most 128 MiB of HBM per device.

v0:
```python
import jax
import jax.numpy as jnp
from jax import lax
from jax.sharding import PartitionSpec as P


def shards(
    tokens,
    tenant_ids,
    placement,
    base_weight,
    delta_levels,
    delta_scales,
    outlier_index,
    outlier_values,
):
    wide_count = lax.axis_size("wide")
    row_count = tenant_ids.shape[0]
    capacity = 5 * row_count // (2 * wide_count)
    positions = jnp.arange(row_count, dtype=jnp.int32)
    same_tenant = tenant_ids[:, None] == tenant_ids[None, :]
    earlier = positions[None, :] < positions[:, None]
    row_rank = jnp.sum((same_tenant & earlier).astype(jnp.int32), axis=1)
    devices = jnp.arange(wide_count, dtype=jnp.int32)
    holds_tenant = tenant_ids[:, None] == placement[None, :]
    holders = jnp.sum(holds_tenant.astype(jnp.int32), axis=1)
    same_peer = placement[:, None] == placement[None, :]
    before = devices[None, :] < devices[:, None]
    peer_rank = jnp.sum((same_peer & before).astype(jnp.int32), axis=1)
    replica = row_rank % holders
    target = holds_tenant & (peer_rank[None, :] == replica[:, None])
    holder_index = jnp.sum(jnp.where(target, devices[None, :], 0), axis=1)
    slot_index = holder_index * capacity + row_rank // holders
    source_row = (
        jnp.full((wide_count * capacity,), row_count, jnp.int32).at[slot_index].set(positions)
    )
    whole = lax.all_gather(tokens, "narrow", axis=1, tiled=True)
    base_part = jnp.dot(whole, base_weight, preferred_element_type=jnp.float32)
    levels = delta_levels[0]
    scales = delta_scales[0]
    picked_cols = outlier_index[0]
    outlier_rows = outlier_values[0]
    outgoing = jnp.take(whole, source_row, axis=0, mode="fill", fill_value=0).reshape(
        wide_count, capacity, whole.shape[1]
    )
    received = lax.all_to_all(outgoing, "wide", split_axis=0, concat_axis=0, tiled=True)
    product = (
        jnp.einsum("nid,df->nif", received, levels, preferred_element_type=jnp.float32) * scales
    )
    chosen = jnp.take(received, picked_cols, axis=2)
    product = product + jnp.einsum(
        "nik,kf->nif", chosen, outlier_rows, preferred_element_type=jnp.float32
    )
    returned_rows = lax.all_to_all(
        product.astype(jnp.bfloat16), "wide", split_axis=0, concat_axis=0, tiled=True
    )
    update = jnp.take(
        returned_rows.reshape(wide_count * capacity, returned_rows.shape[2]), slot_index, axis=0
    )
    return (base_part + update.astype(jnp.float32)).astype(jnp.bfloat16)


def solution(mesh):
    placed = (
        P(("groups", "wide"), "narrow"),
        P("wide"),
        P(),
        P(None, "narrow"),
        P("wide", None, "narrow"),
        P("wide", "narrow"),
        P("wide", None),
        P("wide", None, "narrow"),
    )
    return jax.shard_map(
        shards,
        mesh=mesh,
        in_specs=placed,
        out_specs=P(("groups", "wide"), "narrow"),
        check_vma=False,
    )
```

profile of v0, /device:TPU:0, one launch (start us, length us, event | category | flops | bytes accessed | tf_op | source)
XLA Modules:
  0.0 288.3 jit_solution(7197777051578327804)
XLA Ops:
  6.5 0.0 copy-start
  6.5 0.0 all-gather.2.cloned.1.call-start
  6.5 0.7 all-gather.2.cloned.1.call-update
  7.3 0.9 convert_reduce_fusion.1
  8.2 0.8 fusion.10
  8.9 0.9 convert_reduce_fusion
  9.9 0.1 and_select_fusion
  10.0 0.8 select_reduce_fusion
  10.8 0.1 compare_and_fusion.3
  11.0 1.2 scatter_custom_fusion
  12.2 0.1 broadcast_in_dim.72
  12.3 27.9 %all-gather.2.cloned.1.call-done = bf16[192,8192]{1,0:T(8,128)(2,1)} async-done(((bf16[192,2048]{1,0:T(8,128)(2,1)}), bf16[192,8192]{1,0:T(8,128)(2,1)}) %all-gather.2.cloned.1.call-update) | async-done | bytes 3145744 | tf_op jit(solution)/shard_map/all_gather | solution.py:37
  40.2 17.7 %gather_fusion = bf16[480,8192]{1,0:T(8,128)(2,1)} fusion(bf16[192,8192]{1,0:T(8,128)(2,1)} %all-gather.2.cloned.1.call-done, s32[1024]{0:T(1024)S(1)} %pad_clamp_fusion.2), kind=kCustom, calls=%fused_computation | custom fusion | bytes 15730560 | tf_op jit(solution)/shard_map/jit(_take)/gather | solution.py:43
  57.8 6.9 %broadcast_select_fusion = bf16[4,120,8192]{2,1,0:T(8,128)(2,1)} fusion(bf16[4,120,8192]{2,1,0:T(8,128)(2,1)} %bitcast.27, pred[4,120]{1,0:T(4,128)(4,1)S(1)} %broadcast_in_dim.72), kind=kLoop, calls=%fused_computation.4 | loop fusion | flops 3932160 | bytes 15729120 | tf_op jit(solution)/shard_map/jit(_take)/select_n | solution.py:43
  64.7 0.0 copy-start.2
  64.7 5.9 %all-to-all-start = ((bf16[4,120,8192]{2,1,0:T(8,128)(2,1)}), bf16[4,120,8192]{2,1,0:T(8,128)(2,1)}, u32[]{:S(2)}, u32[]{:S(2)}) async-start(bf16[4,120,8192]{2,1,0:T(8,128)(2,1)} %broadcast_select_fusion), calls=%async_computation | async-start | bytes 15728640 | tf_op jit(solution)/shard_map/all_to_all | solution.py:46
  70.6 0.0 copy-done.2
  70.7 0.0 copy-start.3
  70.7 172.3 %all-to-all-done = bf16[4,120,8192]{2,1,0:T(8,128)(2,1)} async-done(((bf16[4,120,8192]{2,1,0:T(8,128)(2,1)}), bf16[4,120,8192]{2,1,0:T(8,128)(2,1)}, u32[]{:S(2)}, u32[]{:S(2)}) %all-to-all-start) | async-done | bytes 7864352 | tf_op jit(solution)/shard_map/all_to_all | solution.py:46
  243.0 13.5 %copy.11 = bf16[4,120,8192]{1,0,2:T(4,128)(2,1)} copy(bf16[4,120,8192]{2,1,0:T(8,128)(2,1)} %all-to-all-done) | data formatting | bytes 15728640 | tf_op jit(solution)/shard_map/all_to_all | solution.py:46
  256.5 0.0 copy-start.1
  256.5 4.1 %gather_fusion.1 = bf16[128,4,120]{2,1,0:T(4,128)(2,1)S(1)} fusion(bf16[4,120,8192]{1,0,2:T(4,128)(2,1)} %copy.11, s32[1024]{0:T(1024)S(1)} %pad_clamp_fusion.1), kind=kCustom, calls=%fused_computation.1 | custom fusion | bytes 246272 | tf_op jit(solution)/shard_map/jit(_take)/gather | solution.py:50
  260.7 0.2 select_bitcast_fusion
  260.9 0.0 copy-done
  260.9 0.0 copy-done.3
  260.9 5.4 %fusion.2 = f32[4,120,128]{2,1,0:T(8,128)S(1)} fusion(bf16[4,120,8192]{2,1,0:T(8,128)(2,1)} %all-to-all-done, bf16[1,8192,128]{2,1,0:T(8,128)(2,1)S(1)} %copy-done, f32[128]{0:T(128)S(1)} %bitcast.33), kind=kOutput, calls=%fused_computation.7 | convolution fusion | flops 1006694400 | bytes 10207744 | tf_op jit(solution)/shard_map/nid,df->nif/dot_general | solution.py:48
  266.4 0.0 copy-done.1
  266.4 0.9 fusion.5
  267.3 3.3 %all-to-all-start.1 = ((bf16[4,120,128]{2,1,0:T(8,128)(2,1)}), bf16[4,120,128]{2,1,0:T(8,128)(2,1)S(1)}, u32[]{:S(2)}, u32[]{:S(2)}) async-start(bf16[4,120,128]{2,1,0:T(8,128)(2,1)} %fusion.5), calls=%async_computation.1 | async-start | bytes 245760 | tf_op jit(solution)/shard_map/all_to_all | solution.py:54
  270.6 5.9 %all-to-all-done.1 = bf16[4,120,128]{2,1,0:T(8,128)(2,1)S(1)} async-done(((bf16[4,120,128]{2,1,0:T(8,128)(2,1)}), bf16[4,120,128]{2,1,0:T(8,128)(2,1)S(1)}, u32[]{:S(2)}, u32[]{:S(2)}) %all-to-all-start.1) | async-done | bytes 122912 | tf_op jit(solution)/shard_map/all_to_all | solution.py:54
  276.5 0.8 gather_fusion.2
  277.3 4.1 %fusion.6 = bf16[192,128]{1,0:T(8,128)(2,1)} fusion(bf16[192,8192]{1,0:T(8,128)(2,1)} %all-gather.2.cloned.1.call-done, bf16[8192,128]{1,0:T(8,128)(2,1)} %param.11, bf16[192,128]{1,0:T(8,128)(2,1)S(1)} %gather_fusion.2, pred[192]{0:T(512)(128)(4,1)S(1)} %get-tuple-element.5), kind=kOutput, calls=%fused_computation.11 | convolution fusion | flops 402751488 | bytes 5341376 | tf_op jit(solution)/shard_map/dot_general | solution.py:38
  (10 shorter events, 0.1 us)
Async XLA Ops:
  6.5 254.4 %copy-start = (bf16[1,8192,128]{2,1,0:T(8,128)(2,1)S(1)}, bf16[1,8192,128]{2,1,0:T(8,128)(2,1)}, u32[]{:S(2)}) copy-start(bf16[1,8192,128]{2,1,0:T(8,128)(2,1)} %param.12) | copy-start | bytes 6291460
  6.5 33.6 %all-gather.2.cloned.1.call-start = ((), (), s32[]{:S(2)}) async-start(), calls=%async_computation.2 | async-start | bytes 3932160 | tf_op jit(solution)/shard_map/all_gather | solution.py:37
  64.7 5.9 %copy-start.2 = (s32[1,128]{1,0:T(1,128)S(1)}, s32[1,128]{1,0:T(1,128)}, u32[]{:S(2)}) copy-start(s32[1,128]{1,0:T(1,128)} %param.14) | copy-start | bytes 1540
  64.7 178.3 %all-to-all-start = ((bf16[4,120,8192]{2,1,0:T(8,128)(2,1)}), bf16[4,120,8192]{2,1,0:T(8,128)(2,1)}, u32[]{:S(2)}, u32[]{:S(2)}) async-start(bf16[4,120,8192]{2,1,0:T(8,128)(2,1)} %broadcast_select_fusion), calls=%async_computation | async-start | bytes 15728640 | tf_op jit(solution)/shard_map/all_to_all | solution.py:46
  70.7 190.2 %copy-start.3 = (f32[1,128]{1,0:T(1,128)S(1)}, f32[1,128]{1,0:T(1,128)}, u32[]{:S(2)}) copy-start(f32[1,128]{1,0:T(1,128)} %param.13) | copy-start | bytes 1540
  256.5 9.8 %copy-start.1 = (bf16[1,128,128]{2,1,0:T(8,128)(2,1)S(1)}, bf16[1,128,128]{2,1,0:T(8,128)(2,1)}, u32[]{:S(2)}) copy-start(bf16[1,128,128]{2,1,0:T(8,128)(2,1)} %param.15) | copy-start | bytes 98308
  267.3 9.3 %all-to-all-start.1 = ((bf16[4,120,128]{2,1,0:T(8,128)(2,1)}), bf16[4,120,128]{2,1,0:T(8,128)(2,1)S(1)}, u32[]{:S(2)}, u32[]{:S(2)}) async-start(bf16[4,120,128]{2,1,0:T(8,128)(2,1)} %fusion.5), calls=%async_computation.1 | async-start | bytes 245760 | tf_op jit(solution)/shard_map/all_to_all | solution.py:54
Sparse Core Ops, SparseCore 0:
  8.9 31.2 all-gather.1
where the time goes:
time: 289 us; the launch traced here: 288 us
  waiting for transfers between devices  207 us (72%)
  local copies, waits for them, and re-layouts  37.4 us (13%)
  between operations  13.5 us (5%)
  other arithmetic  10.8 us (4%)
  matrix products  10.5 us (4%)
  starting transfers between devices  9.22 us (3%)
    all_to_all x1, waiting for transfers between devices, shards(): lax.all_to_all(outgoing, 'wide', split_axis=0, concat_axis=0, tiled=True)  172 us
    all_gather x1, waiting for transfers between devices, shards(): whole = lax.all_gather(tokens, 'narrow', axis=1, tiled=True)  27.9 us
    gather x1, local copies, waits for them, and re-layouts, shards(): jnp.take(whole, source_row, axis=0, mode='fill', fill_value=0)  17.7 us
    all_to_all x1, local copies, waits for them, and re-layouts, shards(): lax.all_to_all(outgoing, 'wide', split_axis=0, concat_axis=0, tiled=True)  13.5 us
    select_n x2, other arithmetic, shards(): jnp.take(whole, source_row, axis=0, mode='fill', fill_value=0)  6.9 us
    all_to_all x1, waiting for transfers between devices, shards(): lax.all_to_all(product.astype(jnp.bfloat16), 'wide', split_axis=0, concat...  5.94 us
    all_to_all x1, starting transfers between devices, shards(): lax.all_to_all(outgoing, 'wide', split_axis=0, concat_axis=0, tiled=True)  5.9 us
  transfers between devices with their start and end apart: 3, of which 3 were waited for; matrix products, arithmetic and copies ran while one was open for 2% of the time, Pallas kernels for 0%

commit v1 on v0

--- a/solution.py
+++ b/solution.py
@@ -1,10 +1,376 @@
+import functools
+
 import jax
 import jax.numpy as jnp
 from jax import lax
+from jax.experimental import pallas as pl
+from jax.experimental.pallas import tpu as pltpu
 from jax.sharding import PartitionSpec as P
 
-
-def shards(
+MESH = pl.DeviceIdType.MESH
+PIECES = 8
+META = 16
+
+
+def kernel(
+    place, tenants, scales, index, values, tok, base, levels, out,
+    x_all, w_all, ext, from_outer, from_inner, to_inner, to_outer, other, other_index,
+    acc_a, acc_b, acc_c,
+    load_sem, tok_sem,
+    outer_recv, inner_recv, y_recv, x_recv, f_recv, c_recv,
+    inner_send, outer_send, y_send, x_send, f_send, c_send,
+):
+    f32, bf16 = jnp.float32, jnp.bfloat16
+    rows, cols = out.shape
+    depth = base.shape[0]
+    keep = values.shape[0]
+    piece = x_all.shape[2]
+    head = keep // 2 + META
+    g = lax.axis_index("groups")
+    w = lax.axis_index("wide")
+    n = lax.axis_index("narrow")
+    n_core = n + 1 - 2 * (n % 2)
+    n_x = (n + 2) % 4
+    n_far = n_x + 1 - 2 * (n_x % 2)
+    low = w // 2 == 0
+    at_end = (w == 0) | (w == 3)
+    interior = (w == 1) | (w == 2)
+    inner = jnp.where(low, w + 1, w - 1)
+    outer = jnp.where(interior, jnp.where(low, w - 1, w + 1), w)
+    y = 1 - g
+
+    load_levels = pltpu.make_async_copy(levels, w_all.at[:, pl.ds(cols, cols)], load_sem.at[0])
+    load_base = pltpu.make_async_copy(base, w_all.at[:, pl.ds(0, cols)], load_sem.at[1])
+
+    def load_tok(j):
+        return pltpu.make_async_copy(
+            tok.at[:, pl.ds(j * piece, piece)], x_all.at[n * PIECES + j], tok_sem.at[j]
+        )
+
+    for j in range(PIECES):
+        load_tok(j).start()
+    load_levels.start()
+    load_base.start()
+
+    barrier = pltpu.get_barrier_semaphore()
+    for peer in ({"narrow": n_core}, {"narrow": n_x}, {"groups": y}, {"wide": inner}):
+        pl.semaphore_signal(barrier, inc=1, device_id=peer, device_id_type=MESH)
+
+    @pl.when(interior)
+    def _():
+        pl.semaphore_signal(barrier, inc=1, device_id={"wide": outer}, device_id_type=MESH)
+
+    ext[pl.ds(0, keep // 2), :] = values[pl.ds(pl.multiple_of(g * (keep // 2), keep // 2), keep // 2), :]
+    scale = scales[...]
+    top = scale.astype(bf16).astype(f32)
+    mid = (scale - top).astype(bf16).astype(f32)
+    last = scale - top - mid
+    own_index = index[...]
+    index_high = (own_index // 128).astype(f32)
+    index_low = (own_index % 128).astype(f32)
+    line = lax.broadcasted_iota(jnp.int32, (META, cols), 0)
+    meta = jnp.zeros((META, cols), f32)
+    for i, value in enumerate((top, mid, last, index_high, index_low)):
+        meta = jnp.where(line == i, value, meta)
+    ext[pl.ds(keep // 2, META), :] = meta.astype(bf16)
+
+    acc_a[...] = jnp.zeros_like(acc_a)
+    acc_b[...] = jnp.zeros_like(acc_b)
+    acc_c[...] = jnp.zeros_like(acc_c)
+
+    @pl.when(interior)
+    def _():
+        pl.semaphore_wait(barrier, 5)
+
+    @pl.when(at_end)
+    def _():
+        pl.semaphore_wait(barrier, 4)
+
+    def remote(src, dst, send, recv, peer):
+        return pltpu.make_async_remote_copy(
+            src_ref=src, dst_ref=dst, send_sem=send, recv_sem=recv, device_id=peer, device_id_type=MESH
+        )
+
+    def span(q):
+        if isinstance(q, int) and q < 0:
+            return pl.ds(0, head)
+        return pl.ds(pl.multiple_of(head + q * piece, 16), piece)
+
+    def number(half, q):
+        return (2 * half + q % 2) * PIECES + q // 2
+
+    def own_ref(q):
+        if isinstance(q, int) and q < 0:
+            return ext
+        at = pl.multiple_of(number(g, q) * piece, piece)
+        return w_all.at[pl.ds(at, piece), pl.ds(cols, cols)]
+
+    def blast(q):
+        return remote(own_ref(q), from_outer.at[span(q)], inner_send.at[q + 1], outer_recv.at[q + 1], {"wide": inner})
+
+    def send_inner(q):
+        return remote(
+            to_inner.at[span(q)], from_inner.at[span(q)], inner_send.at[q + 1], inner_recv.at[q + 1], {"wide": inner}
+        )
+
+    def send_outer(q):
+        return remote(
+            to_outer.at[span(q)], from_inner.at[span(q)], outer_send.at[q + 1], inner_recv.at[q + 1], {"wide": outer}
+        )
+
+    def send_y(q):
+        return remote(
+            other.at[g, span(q)], other.at[g, span(q)], y_send.at[q + 1], y_recv.at[q + 1], {"groups": y}
+        )
+
+    def send_x(j):
+        at = n * PIECES + j
+        return remote(x_all.at[at], x_all.at[at], x_send.at[j], x_recv.at[j], {"narrow": n_x})
+
+    def send_far(j):
+        at = n_x * PIECES + j
+        return remote(x_all.at[at], x_all.at[at], f_send.at[j], f_recv.at[j], {"narrow": n_core})
+
+    own_slice = x_all.at[pl.ds(n * PIECES, PIECES)]
+    send_core = remote(own_slice, own_slice, c_send, c_recv, {"narrow": n_core})
+
+    def arrived(dst, sem):
+        pltpu.make_async_copy(dst, dst, sem).wait()
+
+    mine = place[w]
+    inner_differs = mine != place[inner]
+    outer_differs = mine != place[outer]
+    total = 2 * PIECES
+
+    @pl.when(at_end)
+    def _():
+        blast(-1).start()
+
+    load_tok(0).wait()
+    send_x(0).start()
+    load_levels.wait()
+
+    @pl.when(at_end)
+    def _():
+        def one(q, carry):
+            blast(q).start()
+            return carry
+        lax.fori_loop(0, total, one, 0)
+
+    for j in range(1, PIECES):
+        load_tok(j).wait()
+        send_x(j).start()
+    send_core.start()
+    load_base.wait()
+
+    def near(q):
+        @pl.when(interior)
+        def _():
+            arrived(from_outer.at[span(q)], outer_recv.at[q + 1])
+            to_inner[span(q), :] = jnp.where(inner_differs, own_ref(q)[...], from_outer[span(q), :])
+            send_inner(q).start()
+
+    def far(q):
+        arrived(from_inner.at[span(q)], inner_recv.at[q + 1])
+
+        @pl.when(interior)
+        def _():
+            to_outer[span(q), :] = jnp.where(outer_differs, own_ref(q)[...], from_inner[span(q), :])
+            send_outer(q).start()
+            other[g, span(q), :] = jnp.where(outer_differs, from_outer[span(q), :], from_inner[span(q), :])
+
+        @pl.when(at_end)
+        def _():
+            other[g, span(q), :] = from_inner[span(q), :]
+
+        send_y(q).start()
+
+    line_piece = lax.broadcasted_iota(jnp.int32, (piece, keep), 0)
+
+    def picks(p, which):
+        return (line_piece + p * piece == which).astype(f32).astype(bf16)
+
+    def local(p):
+        x = x_all[p]
+        at = pl.multiple_of(p * piece, piece)
+        acc_a[...] += jnp.dot(x, w_all[pl.ds(at, piece), :], preferred_element_type=f32)
+        acc_c[...] += jnp.dot(x, picks(p, index[...]), preferred_element_type=f32)
+
+    def foreign(half, q):
+        p = number(half, q)
+        both = jnp.concatenate([other[half, span(q), :], picks(p, other_index[...])], axis=1)
+        acc_b[...] += jnp.dot(x_all[p], both, preferred_element_type=f32)
+
+    def step(d):
+        traced = not isinstance(d, int)
+        if traced or d < PIECES:
+            if not traced and d == 0:
+                near(-1)
+            near(2 * d)
+            near(2 * d + 1)
+        if traced or 1 <= d <= PIECES:
+            if not traced and d == 1:
+                far(-1)
+                info = other[g, pl.ds(keep // 2, META), :].astype(f32)
+                other_index[...] = (info[3:4] * 128.0 + info[4:5]).astype(jnp.int32)
+            far(2 * d - 2)
+            far(2 * d - 1)
+        if traced or d < PIECES:
+            arrived(x_all.at[n_x * PIECES + d], x_recv.at[d])
+            send_far(d).start()
+            local(n * PIECES + d)
+            if not traced and d == 0:
+                arrived(x_all.at[pl.ds(n_core * PIECES, PIECES)], c_recv)
+            local(n_core * PIECES + d)
+            local(n_x * PIECES + d)
+        if traced or 1 <= d <= PIECES:
+            arrived(x_all.at[n_far * PIECES + d - 1], f_recv.at[d - 1])
+            local(n_far * PIECES + d - 1)
+        if traced or d >= 2:
+            for q in (2 * d - 4, 2 * d - 3):
+                foreign(g, q)
+            for q in (2 * d - 4, 2 * d - 3):
+                arrived(other.at[y, span(q)], y_recv.at[q + 1])
+                foreign(y, q)
+
+    step(0)
+    step(1)
+
+    def middle(d, carry):
+        step(d)
+        return carry
+
+    lax.fori_loop(2, PIECES, middle, 0)
+    step(PIECES)
+    step(PIECES + 1)
+    arrived(other.at[y, span(-1)], y_recv.at[0])
+
+    info = other[g, pl.ds(keep // 2, META), :].astype(f32)
+    other_scale = info[0:1] + info[1:2] + info[2:3]
+    other_values = jnp.concatenate(
+        [other[0, pl.ds(0, keep // 2), :], other[1, pl.ds(0, keep // 2), :]], axis=0
+    )
+    own_update = acc_a[:, pl.ds(cols, cols)] * scale + jnp.dot(
+        acc_c[...].astype(bf16), values[...], preferred_element_type=f32
+    )
+    other_update = acc_b[:, pl.ds(0, cols)] * other_scale + jnp.dot(
+        acc_b[:, pl.ds(cols, keep)].astype(bf16), other_values, preferred_element_type=f32
+    )
+    square = (rows, rows)
+    diagonal = lax.broadcasted_iota(jnp.int32, square, 0) == lax.broadcasted_iota(jnp.int32, square, 1)
+    belongs = jnp.where(diagonal & (tenants[...] == mine), 1.0, 0.0)
+    is_own = jnp.sum(belongs, axis=1, keepdims=True) > 0.5
+    update = jnp.where(is_own, own_update, other_update).astype(bf16)
+    out[...] = (acc_a[:, pl.ds(0, cols)] + update.astype(f32)).astype(bf16)
+
+    def sent(copy):
+        copy.wait_send()
+
+    def ends(q, carry):
+        sent(blast(q))
+        return carry
+
+    def middles(q, carry):
+        sent(send_inner(q))
+        sent(send_outer(q))
+        return carry
+
+    def alls(q, carry):
+        sent(send_y(q))
+        return carry
+
+    def slices(j, carry):
+        sent(send_x(j))
+        sent(send_far(j))
+        return carry
+
+    @pl.when(at_end)
+    def _():
+        sent(blast(-1))
+        lax.fori_loop(0, total, ends, 0)
+
+    @pl.when(interior)
+    def _():
+        sent(send_inner(-1))
+        sent(send_outer(-1))
+        lax.fori_loop(0, total, middles, 0)
+
+    sent(send_y(-1))
+    lax.fori_loop(0, total, alls, 0)
+    lax.fori_loop(0, PIECES, slices, 0)
+    sent(send_core)
+
+
+def delta_plan(
+    tokens,
+    tenant_ids,
+    placement,
+    base_weight,
+    delta_levels,
+    delta_scales,
+    outlier_index,
+    outlier_values,
+):
+    rows, width = tokens.shape
+    depth, cols = base_weight.shape
+    keep = outlier_index.shape[1]
+    piece = width // PIECES
+    slices = depth // width
+    stream = keep // 2 + META + depth // 2
+    parts = 2 * PIECES + 1
+    bf16 = jnp.bfloat16
+    vmem = pl.BlockSpec(memory_space=pltpu.VMEM)
+    hbm = pl.BlockSpec(memory_space=pl.ANY)
+    dma = pltpu.SemaphoreType.DMA
+    return pl.pallas_call(
+        kernel,
+        out_shape=jax.ShapeDtypeStruct((rows, cols), bf16),
+        in_specs=[pl.BlockSpec(memory_space=pltpu.SMEM), vmem, vmem, vmem, vmem, hbm, hbm, hbm],
+        out_specs=vmem,
+        scratch_shapes=[
+            pltpu.VMEM((slices * PIECES, rows, piece), bf16),
+            pltpu.VMEM((depth, 2 * cols), bf16),
+            pltpu.VMEM((keep // 2 + META, cols), bf16),
+            pltpu.VMEM((stream, cols), bf16),
+            pltpu.VMEM((stream, cols), bf16),
+            pltpu.VMEM((stream, cols), bf16),
+            pltpu.VMEM((stream, cols), bf16),
+            pltpu.VMEM((2, stream, cols), bf16),
+            pltpu.VMEM((1, keep), jnp.int32),
+            pltpu.VMEM((rows, 2 * cols), jnp.float32),
+            pltpu.VMEM((rows, cols + keep), jnp.float32),
+            pltpu.VMEM((rows, keep), jnp.float32),
+            dma((2,)),
+            dma((PIECES,)),
+            dma((parts,)),
+            dma((parts,)),
+            dma((parts,)),
+            dma((PIECES,)),
+            dma((PIECES,)),
+            dma,
+            dma((parts,)),
+            dma((parts,)),
+            dma((parts,)),
+            dma((PIECES,)),
+            dma((PIECES,)),
+            dma,
+        ],
+        compiler_params=pltpu.CompilerParams(
+            collective_id=0, has_side_effects=True, vmem_limit_bytes=40 * 1024 * 1024
+        ),
+    )(
+        placement,
+        tenant_ids.reshape(1, rows),
+        delta_scales,
+        outlier_index,
+        outlier_values[0],
+        tokens,
+        base_weight,
+        delta_levels[0],
+    )
+
+
+def row_plan(
     tokens,
     tenant_ids,
     placement,
@@ -71,8 +437,9 @@
         P("wide", None),
         P("wide", None, "narrow"),
     )
+    few = mesh.shape["wide"] == 4 and mesh.shape["narrow"] == 4 and mesh.shape["groups"] == 2
     return jax.shard_map(
-        shards,
+        delta_plan if few else row_plan,
         mesh=mesh,
         in_specs=placed,
         out_specs=P(("groups", "wide"), "narrow"),

time: 289 us -> 53.8 us (0.19)
  waiting for transfers between devices: 207 us -> 0 us
  Pallas kernels: 0 us -> 45.1 us
  local copies, waits for them, and re-layouts: 37.4 us -> 8.34 us
  between operations: 13.5 us -> 0.02 us
  other arithmetic: 10.8 us -> 0 us
  matrix products: 10.5 us -> 0 us
  starting transfers between devices: 9.22 us -> 0 us
    all_to_all x2 -> x0, waiting for transfers between devices: 178 us -> none  [the longest x1 172 us: shards(): lax.all_to_all(outgoing, 'wide', split_axis=0, concat_axis=0, tiled=True)]
    pallas_call x0 -> x1, Pallas kernels: none -> 45.1 us  [delta_plan(): pl.pallas_call(kernel, out_shape=jax.ShapeDtypeStruct((rows, cols), bf16)...]
    all_gather x1 -> x0, waiting for transfers between devices: 27.9 us -> none  [shards(): whole = lax.all_gather(tokens, 'narrow', axis=1, tiled=True)]
    gather x3 -> x0, local copies, waits for them, and re-layouts: 22.6 us -> none  [the longest x1 17.7 us: shards(): jnp.take(whole, source_row, axis=0, mode='fill', fill_value=0)]
    all_to_all x1 -> x0, local copies, waits for them, and re-layouts: 13.5 us -> none  [shards(): lax.all_to_all(outgoing, 'wide', split_axis=0, concat_axis=0, tiled=True)]
    dot_general x3 -> x0, matrix products: 10.5 us -> none  [the longest x1 5.44 us: shards(): jnp.einsum('nid,df->nif', received, levels, preferred_element_type=jnp.fl...]
    all_to_all x2 -> x0, starting transfers between devices: 9.22 us -> none  [the longest x1 5.9 us: shards(): lax.all_to_all(outgoing, 'wide', split_axis=0, concat_axis=0, tiled=True)]
    unnamed x8 -> x17, local copies, waits for them, and re-layouts: 0.02 us -> 8.34 us
  transfers between devices with their start and end apart: 3 -> 0, of which waited for: 3 -> 0; matrix products, arithmetic and copies ran while one was open for 2% -> 0% of each run, Pallas kernels for 0% -> 0%
where the time goes in v1:
time: 53.8 us; the launch traced here: 53.5 us
  Pallas kernels  45.1 us (84%)
  local copies, waits for them, and re-layouts  8.34 us (16%)
    pallas_call x1, Pallas kernels, delta_plan(): pl.pallas_call(kernel, out_shape=jax.ShapeDtypeStruct((rows, cols), bf16)...  45.1 us
    unnamed x17, local copies, waits for them, and re-layouts  8.34 us

profile of v1, /device:TPU:0, one launch (start us, length us, event | category | flops | bytes accessed | tf_op | source)
XLA Modules:
  0.0 53.5 jit_solution(17989819062746992755)
XLA Ops:
  0.0 0.0 copy-start
  0.0 1.6 %copy-done = bf16[8192,128]{1,0:T(8,128)(2,1)S(1)} copy-done((bf16[8192,128]{1,0:T(8,128)(2,1)S(1)}, bf16[8192,128]{1,0:T(8,128)(2,1)}, u32[]{:S(2)}) %copy-start) | copy-done | bytes 2097176
  1.6 0.0 copy-start.1
  1.6 1.6 %copy-done.1 = bf16[1,8192,128]{2,1,0:T(8,128)(2,1)S(1)} copy-done((bf16[1,8192,128]{2,1,0:T(8,128)(2,1)S(1)}, bf16[1,8192,128]{2,1,0:T(8,128)(2,1)}, u32[]{:S(2)}) %copy-start.1) | copy-done | bytes 2097176
  3.2 0.0 copy-start.2
  3.2 1.1 %copy-done.2 = bf16[192,2048]{1,0:T(8,128)(2,1)S(1)} copy-done((bf16[192,2048]{1,0:T(8,128)(2,1)S(1)}, bf16[192,2048]{1,0:T(8,128)(2,1)}, u32[]{:S(2)}) %copy-start.2) | copy-done | bytes 786456
  4.3 0.0 copy-start.3
  4.3 0.8 %copy-done.3 = bf16[1,128,128]{2,1,0:T(8,128)(2,1)S(1)} copy-done((bf16[1,128,128]{2,1,0:T(8,128)(2,1)S(1)}, bf16[1,128,128]{2,1,0:T(8,128)(2,1)}, u32[]{:S(2)}) %copy-start.3) | copy-done | bytes 32792
  5.1 0.0 copy-start.4
  5.1 0.7 %copy-done.4 = s32[192]{0:T(256)S(1)} copy-done((s32[192]{0:T(256)S(1)}, s32[192]{0:T(256)}, u32[]{:S(2)}) %copy-start.4) | copy-done | bytes 792
  5.8 0.0 copy-start.5
  5.8 0.7 %copy-done.5 = s32[4]{0:T(128)S(1)} copy-done((s32[4]{0:T(128)S(1)}, s32[4]{0:T(128)}, u32[]{:S(2)}) %copy-start.5) | copy-done | bytes 40
  6.4 0.0 copy-start.6
  6.4 0.7 %copy-done.6 = f32[1,128]{1,0:T(1,128)S(1)} copy-done((f32[1,128]{1,0:T(1,128)S(1)}, f32[1,128]{1,0:T(1,128)}, u32[]{:S(2)}) %copy-start.6) | copy-done | bytes 536
  7.1 0.0 copy-start.7
  7.1 0.7 %copy-done.7 = s32[1,128]{1,0:T(1,128)S(1)} copy-done((s32[1,128]{1,0:T(1,128)S(1)}, s32[1,128]{1,0:T(1,128)}, u32[]{:S(2)}) %copy-start.7) | copy-done | bytes 536
  7.7 45.1 %shard_map.82 = bf16[192,128]{1,0:T(8,128)(2,1)S(1)} custom-call(s32[4]{0:T(128)S(1)} %copy-done.5, s32[1,192]{1,0:T(1,128)S(1)} %bitcast.5, f32[1,128]{1,0:T(1,128)S(1)} %copy-done.6, s32[1,128]{1,0:T(1,128)S(1)} %copy-done.7, bf16[128,128]{1,0:T(8,128)(2,1)S(1)} %bitcast.4, bf16[192,2048]{1,0:T(8,128)(2,1)S(1)} %copy-done.2, ...), custom_call_target="tpu_custom_call" | custom-call | tf_op jit(solution)/shard_map/pallas_call | solution.py:325
  52.8 0.6 %copy.10 = bf16[192,128]{1,0:T(8,128)(2,1)} copy(bf16[192,128]{1,0:T(8,128)(2,1)S(1)} %shard_map.82) | data formatting | bytes 98304
Async XLA Ops:
  0.0 1.6 %copy-start = (bf16[8192,128]{1,0:T(8,128)(2,1)S(1)}, bf16[8192,128]{1,0:T(8,128)(2,1)}, u32[]{:S(2)}) copy-start(bf16[8192,128]{1,0:T(8,128)(2,1)} %base.1) | copy-start | bytes 6291460
  1.6 1.6 %copy-start.1 = (bf16[1,8192,128]{2,1,0:T(8,128)(2,1)S(1)}, bf16[1,8192,128]{2,1,0:T(8,128)(2,1)}, u32[]{:S(2)}) copy-start(bf16[1,8192,128]{2,1,0:T(8,128)(2,1)} %param.12) | copy-start | bytes 6291460
  3.2 1.1 %copy-start.2 = (bf16[192,2048]{1,0:T(8,128)(2,1)S(1)}, bf16[192,2048]{1,0:T(8,128)(2,1)}, u32[]{:S(2)}) copy-start(bf16[192,2048]{1,0:T(8,128)(2,1)} %tok.1) | copy-start | bytes 2359300
  4.3 0.8 %copy-start.3 = (bf16[1,128,128]{2,1,0:T(8,128)(2,1)S(1)}, bf16[1,128,128]{2,1,0:T(8,128)(2,1)}, u32[]{:S(2)}) copy-start(bf16[1,128,128]{2,1,0:T(8,128)(2,1)} %param.15) | copy-start | bytes 98308
  5.1 0.7 %copy-start.4 = (s32[192]{0:T(256)S(1)}, s32[192]{0:T(256)}, u32[]{:S(2)}) copy-start(s32[192]{0:T(256)} %param.9) | copy-start | bytes 2308
  5.8 0.7 %copy-start.5 = (s32[4]{0:T(128)S(1)}, s32[4]{0:T(128)}, u32[]{:S(2)}) copy-start(s32[4]{0:T(128)} %place.1) | copy-start | bytes 52
  6.4 0.7 %copy-start.6 = (f32[1,128]{1,0:T(1,128)S(1)}, f32[1,128]{1,0:T(1,128)}, u32[]{:S(2)}) copy-start(f32[1,128]{1,0:T(1,128)} %scales.1) | copy-start | bytes 1540
  7.1 0.7 %copy-start.7 = (s32[1,128]{1,0:T(1,128)S(1)}, s32[1,128]{1,0:T(1,128)}, u32[]{:S(2)}) copy-start(s32[1,128]{1,0:T(1,128)} %index.1) | copy-start | bytes 1540

commit v2 on v1

--- a/solution.py
+++ b/solution.py
@@ -356,7 +356,7 @@
             dma,
         ],
         compiler_params=pltpu.CompilerParams(
-            collective_id=0, has_side_effects=True, vmem_limit_bytes=40 * 1024 * 1024
+            collective_id=0, has_side_effects=True, vmem_limit_bytes=64 * 1024 * 1024 - 65536
         ),
     )(
         placement,

time: 53.8 us -> 46.6 us (0.87)
  local copies, waits for them, and re-layouts: 8.34 us -> 1.42 us
    unnamed x17 -> x1, local copies, waits for them, and re-layouts: 8.34 us -> 1.42 us
where the time goes in v2:
time: 46.6 us; the launch traced here: 46.3 us
  Pallas kernels  44.9 us (96%)
  local copies, waits for them, and re-layouts  1.42 us (3%)
    pallas_call x1, Pallas kernels, delta_plan(): pl.pallas_call(kernel, out_shape=jax.ShapeDtypeStruct((rows, cols), bf16)...  44.9 us
    unnamed x1, local copies, waits for them, and re-layouts  1.42 us

profile of v2, /device:TPU:0, one launch (start us, length us, event | category | flops | bytes accessed | tf_op | source)
XLA Modules:
  0.0 46.3 jit_solution(6694914049959982684)
XLA Ops:
  0.0 44.9 %shard_map.82 = bf16[192,128]{1,0:T(8,128)(2,1)} custom-call(s32[4]{0:T(128)} %place.1, s32[1,192]{1,0:T(1,128)} %bitcast.5, f32[1,128]{1,0:T(1,128)} %scales.1, s32[1,128]{1,0:T(1,128)} %index.1, bf16[128,128]{1,0:T(8,128)(2,1)} %bitcast.4, bf16[192,2048]{1,0:T(8,128)(2,1)} %tok.1, bf16[8192,128]{1,0:T(8,128)(2,1)} %base.1, bf16[8192,128]{1,0:T(8,128)(2,1)} %bitcast.3), custom_call_target="tpu_custom_call" | custom-call | tf_op jit(solution)/shard_map/pallas_call | solution.py:325
  44.9 1.4 %copy.10 = bf16[192,128]{1,0:T(8,128)(2,1)} copy(bf16[192,128]{1,0:T(8,128)(2,1)} %shard_map.82) | data formatting | bytes 98304

commit v3 on v2

--- a/solution.py
+++ b/solution.py
@@ -12,13 +12,37 @@
 META = 16
 
 
+def lookup(w, table):
+    value = jnp.int32(table[0])
+    for i in range(1, len(table)):
+        value = jnp.where(w == i, jnp.int32(table[i]), value)
+    return value
+
+
+def routes(same):
+    held = [0]
+    for equal in same:
+        held.append(held[-1] if equal else 1 - held[-1])
+    count = len(held)
+    parent = []
+    for w in range(count):
+        far = [(abs(v - w), v) for v in range(count) if held[v] != held[w]]
+        parent.append(w + 1 if min(far)[1] > w else w - 1)
+    own, passed = {}, {}
+    for name, shift in (("low", -1), ("high", 1)):
+        child = [0 <= w + shift < count and parent[w + shift] == w for w in range(count)]
+        own[name] = [int(child[w] and held[w + shift] != held[w]) for w in range(count)]
+        passed[name] = [int(child[w] and held[w + shift] == held[w]) for w in range(count)]
+    return own, passed
+
+
 def kernel(
-    place, tenants, scales, index, values, tok, base, levels, out,
-    x_all, w_all, ext, from_outer, from_inner, to_inner, to_outer, other, other_index,
+    same, place, tenants, scales, index, values, tok, base, levels, out,
+    x_all, w_all, ext, other, other_index,
     acc_a, acc_b, acc_c,
     load_sem, tok_sem,
-    outer_recv, inner_recv, y_recv, x_recv, f_recv, c_recv,
-    inner_send, outer_send, y_send, x_send, f_send, c_send,
+    z_recv, y_recv, x_recv, f_recv, c_recv,
+    low_send, high_send, y_send, x_send, f_send, c_send,
 ):
     f32, bf16 = jnp.float32, jnp.bfloat16
     rows, cols = out.shape
@@ -105,18 +129,17 @@
         at = pl.multiple_of(number(g, q) * piece, piece)
         return w_all.at[pl.ds(at, piece), pl.ds(cols, cols)]
 
-    def blast(q):
-        return remote(own_ref(q), from_outer.at[span(q)], inner_send.at[q + 1], outer_recv.at[q + 1], {"wide": inner})
-
-    def send_inner(q):
-        return remote(
-            to_inner.at[span(q)], from_inner.at[span(q)], inner_send.at[q + 1], inner_recv.at[q + 1], {"wide": inner}
-        )
-
-    def send_outer(q):
-        return remote(
-            to_outer.at[span(q)], from_inner.at[span(q)], outer_send.at[q + 1], inner_recv.at[q + 1], {"wide": outer}
-        )
+    own_to, pass_to = routes(same)
+    sides = (("low", jnp.maximum(w - 1, 0), low_send), ("high", jnp.minimum(w + 1, 3), high_send))
+
+    def give(side, q):
+        name, peer, sems = side
+        return remote(own_ref(q), other.at[g, span(q)], sems.at[q + 1], z_recv.at[q + 1], {"wide": peer})
+
+    def hand_on(side, q):
+        name, peer, sems = side
+        at = other.at[g, span(q)]
+        return remote(at, at, sems.at[q + 1], z_recv.at[q + 1], {"wide": peer})
 
     def send_y(q):
         return remote(
@@ -138,24 +161,26 @@
         pltpu.make_async_copy(dst, dst, sem).wait()
 
     mine = place[w]
-    inner_differs = mine != place[inner]
-    outer_differs = mine != place[outer]
     total = 2 * PIECES
 
-    @pl.when(at_end)
-    def _():
-        blast(-1).start()
+    for side in sides:
+        if any(own_to[side[0]]):
+            @pl.when(lookup(w, own_to[side[0]]) == 1)
+            def _(side=side):
+                give(side, -1).start()
 
     load_tok(0).wait()
     send_x(0).start()
     load_levels.wait()
 
-    @pl.when(at_end)
-    def _():
-        def one(q, carry):
-            blast(q).start()
-            return carry
-        lax.fori_loop(0, total, one, 0)
+    for side in sides:
+        if any(own_to[side[0]]):
+            @pl.when(lookup(w, own_to[side[0]]) == 1)
+            def _(side=side):
+                def one(q, carry):
+                    give(side, q).start()
+                    return carry
+                lax.fori_loop(0, total, one, 0)
 
     for j in range(1, PIECES):
         load_tok(j).wait()
@@ -163,26 +188,13 @@
     send_core.start()
     load_base.wait()
 
-    def near(q):
-        @pl.when(interior)
-        def _():
-            arrived(from_outer.at[span(q)], outer_recv.at[q + 1])
-            to_inner[span(q), :] = jnp.where(inner_differs, own_ref(q)[...], from_outer[span(q), :])
-            send_inner(q).start()
-
-    def far(q):
-        arrived(from_inner.at[span(q)], inner_recv.at[q + 1])
-
-        @pl.when(interior)
-        def _():
-            to_outer[span(q), :] = jnp.where(outer_differs, own_ref(q)[...], from_inner[span(q), :])
-            send_outer(q).start()
-            other[g, span(q), :] = jnp.where(outer_differs, from_outer[span(q), :], from_inner[span(q), :])
-
-        @pl.when(at_end)
-        def _():
-            other[g, span(q), :] = from_inner[span(q), :]
-
+    def take(q):
+        arrived(other.at[g, span(q)], z_recv.at[q + 1])
+        for side in sides:
+            if any(pass_to[side[0]]):
+                @pl.when(lookup(w, pass_to[side[0]]) == 1)
+                def _(side=side):
+                    hand_on(side, q).start()
         send_y(q).start()
 
     line_piece = lax.broadcasted_iota(jnp.int32, (piece, keep), 0)
@@ -204,31 +216,26 @@
     def step(d):
         traced = not isinstance(d, int)
         if traced or d < PIECES:
+            arrived(x_all.at[n_x * PIECES + d], x_recv.at[d])
+            send_far(d).start()
             if not traced and d == 0:
-                near(-1)
-            near(2 * d)
-            near(2 * d + 1)
-        if traced or 1 <= d <= PIECES:
-            if not traced and d == 1:
-                far(-1)
+                local(n * PIECES)
+                arrived(x_all.at[pl.ds(n_core * PIECES, PIECES)], c_recv)
+                take(-1)
                 info = other[g, pl.ds(keep // 2, META), :].astype(f32)
                 other_index[...] = (info[3:4] * 128.0 + info[4:5]).astype(jnp.int32)
-            far(2 * d - 2)
-            far(2 * d - 1)
-        if traced or d < PIECES:
-            arrived(x_all.at[n_x * PIECES + d], x_recv.at[d])
-            send_far(d).start()
-            local(n * PIECES + d)
-            if not traced and d == 0:
-                arrived(x_all.at[pl.ds(n_core * PIECES, PIECES)], c_recv)
+            take(2 * d)
+            if traced or d > 0:
+                local(n * PIECES + d)
             local(n_core * PIECES + d)
+            take(2 * d + 1)
             local(n_x * PIECES + d)
         if traced or 1 <= d <= PIECES:
             arrived(x_all.at[n_far * PIECES + d - 1], f_recv.at[d - 1])
             local(n_far * PIECES + d - 1)
+            for q in (2 * d - 2, 2 * d - 1):
+                foreign(g, q)
         if traced or d >= 2:
-            for q in (2 * d - 4, 2 * d - 3):
-                foreign(g, q)
             for q in (2 * d - 4, 2 * d - 3):
                 arrived(other.at[y, span(q)], y_recv.at[q + 1])
                 foreign(y, q)
@@ -266,15 +273,6 @@
     def sent(copy):
         copy.wait_send()
 
-    def ends(q, carry):
-        sent(blast(q))
-        return carry
-
-    def middles(q, carry):
-        sent(send_inner(q))
-        sent(send_outer(q))
-        return carry
-
     def alls(q, carry):
         sent(send_y(q))
         return carry
@@ -284,16 +282,17 @@
         sent(send_far(j))
         return carry
 
-    @pl.when(at_end)
-    def _():
-        sent(blast(-1))
-        lax.fori_loop(0, total, ends, 0)
-
-    @pl.when(interior)
-    def _():
-        sent(send_inner(-1))
-        sent(send_outer(-1))
-        lax.fori_loop(0, total, middles, 0)
+    for side in sides:
+        for table, copy in ((own_to, give), (pass_to, hand_on)):
+            if any(table[side[0]]):
+                @pl.when(lookup(w, table[side[0]]) == 1)
+                def _(side=side, copy=copy):
+                    sent(copy(side, -1))
+
+                    def one(q, carry):
+                        sent(copy(side, q))
+                        return carry
+                    lax.fori_loop(0, total, one, 0)
 
     sent(send_y(-1))
     lax.fori_loop(0, total, alls, 0)
@@ -322,8 +321,8 @@
     vmem = pl.BlockSpec(memory_space=pltpu.VMEM)
     hbm = pl.BlockSpec(memory_space=pl.ANY)
     dma = pltpu.SemaphoreType.DMA
-    return pl.pallas_call(
-        kernel,
+    call = lambda same, ident: pl.pallas_call(
+        functools.partial(kernel, same),
         out_shape=jax.ShapeDtypeStruct((rows, cols), bf16),
         in_specs=[pl.BlockSpec(memory_space=pltpu.SMEM), vmem, vmem, vmem, vmem, hbm, hbm, hbm],
         out_specs=vmem,
@@ -331,10 +330,6 @@
             pltpu.VMEM((slices * PIECES, rows, piece), bf16),
             pltpu.VMEM((depth, 2 * cols), bf16),
             pltpu.VMEM((keep // 2 + META, cols), bf16),
-            pltpu.VMEM((stream, cols), bf16),
-            pltpu.VMEM((stream, cols), bf16),
-            pltpu.VMEM((stream, cols), bf16),
-            pltpu.VMEM((stream, cols), bf16),
             pltpu.VMEM((2, stream, cols), bf16),
             pltpu.VMEM((1, keep), jnp.int32),
             pltpu.VMEM((rows, 2 * cols), jnp.float32),
@@ -342,7 +337,6 @@
             pltpu.VMEM((rows, keep), jnp.float32),
             dma((2,)),
             dma((PIECES,)),
-            dma((parts,)),
             dma((parts,)),
             dma((parts,)),
             dma((PIECES,)),
@@ -356,9 +350,16 @@
             dma,
         ],
         compiler_params=pltpu.CompilerParams(
-            collective_id=0, has_side_effects=True, vmem_limit_bytes=64 * 1024 * 1024 - 65536
+            collective_id=ident, has_side_effects=True, vmem_limit_bytes=64 * 1024 * 1024 - 65536
         ),
-    )(
+    )
+
+    ways = [(a, b, c) for a in (False, True) for b in (False, True) for c in (False, True)][:-1]
+    equal = (placement[:-1] == placement[1:]).astype(jnp.int32)
+    which = jnp.minimum(equal[0] * 4 + equal[1] * 2 + equal[2], len(ways) - 1)
+    return lax.switch(
+        which,
+        [call(same, ident) for ident, same in enumerate(ways)],
         placement,
         tenant_ids.reshape(1, rows),
         delta_scales,

time: 46.6 us -> 41.4 us (0.89)
  Pallas kernels: 44.9 us -> 36.1 us
  between operations: 0.01 us -> 1.97 us
  other arithmetic: 0 us -> 0.8 us
  local copies, waits for them, and re-layouts: 1.42 us -> 2.07 us
    pallas_call x1, Pallas kernels: 44.9 us -> 36.1 us  [delta_plan(): lax.switch(which, [call(same, ident) for ident, same in enumerate(ways)],...]
    convert_element_type x0 -> x1, other arithmetic: none -> 0.8 us  [delta_plan(): equal = (placement[:-1] == placement[1:]).astype(jnp.int32)]
    slice x0 -> x1, local copies, waits for them, and re-layouts: none -> 0.65 us  [delta_plan(): which = jnp.minimum(equal[0] * 4 + equal[1] * 2 + equal[2], len(ways) - 1)]
where the time goes in v3:
time: 41.4 us; the launch traced here: 41.2 us
  Pallas kernels  36.1 us (87%)
  local copies, waits for them, and re-layouts  2.07 us (5%)
  between operations  1.97 us (5%)
  other arithmetic  0.8 us (2%)
    pallas_call x1, Pallas kernels, delta_plan(): lax.switch(which, [call(same, ident) for ident, same in enumerate(ways)],...  36.1 us
    unnamed x1, local copies, waits for them, and re-layouts  1.42 us

profile of v3, /device:TPU:0, one launch (start us, length us, event | category | flops | bytes accessed | tf_op | source)
XLA Modules:
  0.0 41.2 jit_solution(11227943607604228465)
XLA Ops:
  0.0 0.8 %compare_convert_fusion = s32[3]{0:T(128)S(1)} fusion(s32[4]{0:T(128)} %param.17), kind=kLoop, calls=%fused_computation | loop fusion | flops 6 | bytes 36 | tf_op jit(solution)/shard_map/convert_element_type | solution.py:358
  0.8 0.7 %fusion = (s32[1]{0:T(128)}, s32[1]{0:T(128)}, s32[1]{0:T(128)}) fusion(s32[3]{0:T(128)S(1)} %compare_convert_fusion), kind=kLoop, calls=%fused_computation.1 | loop fusion | bytes 24 | tf_op jit(solution)/shard_map/slice | solution.py:359
  3.4 36.3 %conditional.1 = (bf16[192,128]{1,0:T(8,128)(2,1)}) conditional(s32[]{:T(128)} %bitcast, (s32[4]{0:T(128)}, s32[1,192]{1,0:T(1,128)}, f32[1,128]{1,0:T(1,128)}, s32[1,128]{1,0:T(1,128)}, bf16[128,128]{1,0:T(8,128)(2,1)}, /*index=5*/bf16[192,2048]{1,0:T(8,128)(2,1)}, bf16[8192,128]{1,0:T(8,128)(2,1)}, ...), branch_computations={%region_0.0_spmd, %region_1.0_spmd, %region_2.0_spmd, %region_3.0_... | conditional | bytes 8 | solution.py:360
  3.4 36.1 %branch_0_fun.1 = bf16[192,128]{1,0:T(8,128)(2,1)} custom-call(s32[4]{0:T(128)} %get-tuple-element.112.place, s32[1,192]{1,0:T(1,128)} %get-tuple-element.114.tenants, f32[1,128]{1,0:T(1,128)} %get-tuple-element.116.scales, s32[1,128]{1,0:T(1,128)} %get-tuple-element.126.index, bf16[128,128]{1,0:T(8,128)(2,1)} %get-tuple-element.128.values, ...), custom_call_target="tpu_custom_call" | custom-call | tf_op jit(solution)/shard_map/cond/branch_0_fun/pallas_call | solution.py:360
  39.8 1.4 %copy.24 = bf16[192,128]{1,0:T(8,128)(2,1)} copy(bf16[192,128]{1,0:T(8,128)(2,1)} %get-tuple-element.181) | data formatting | bytes 98304
